TPU v7x, 512 devices: a whole 4x4x16 slice. The times are simulated.
512 devices in a mesh: radial: 4 (over x), mode: 128 (over z, y, core).
Axes of the slice: x: 4, y: 4, z: 16, core: 2. Of those that a mesh axis runs over, the one named last changes fastest.
Arguments:
- spectral_state: float32 [256, 3, 8, 2, 513], P('mode', None, 'radial'), may hold values from -6 to 6
- synthesis_table: bfloat16 [256, 513, 512], P('mode', None, 'radial'), may hold values from -0.0078125 to 0.0078125
- low_orders: int32 [256], replicated, may hold values from 0 to 255, each once
- diffusion: float32 [3], replicated, may hold values from 200 to 2000
- coupling: float32 [3], replicated, may hold values from 1 to 4
Outputs:
- updated: float32 [256, 3, 8, 2, 513], P('mode', None, 'radial')
Inputs may be any that keep to these rules, and one draw needn't show every extreme that they name: A permutation: pair j holds the orders low_orders[j] and 511 - low_orders[j].
All inputs are finite; a program needn't handle non-finite values.
Results may differ from a plain program's by a relative error of at most 0.0023.
The roundings to bfloat16 on the way count: a program that leaves them out, or rounds other values in their place, can miss the bound.
Values may be sent and summed in bfloat16 or wider, within the bound.
A program may use at most 64 MiB of HBM per device.

v0:
```python
import math

import jax
import jax.numpy as jnp
import ml_dtypes
import numpy as np
from jax import lax
from jax.experimental import pallas as pl
from jax.experimental.pallas import tpu as pltpu
from jax.sharding import PartitionSpec as P

inner_radius = 0.538
shell_step = 1.0 / 2048.0

ORDERS = 512
HALF = 256
ROWS = 513
PADDED = 640
NLON = 1536
QUARTER = 384
NLAT = 1024
SLABS = 4
NEAR = 8
FAR = 16
KAPPA = 2.0 * math.sqrt(ORDERS * (ORDERS + 1) / (NLAT * NLON))
MESH = pl.DeviceIdType.MESH
F32 = jnp.float32
BF16 = jnp.bfloat16


def wave_tables():
    low = np.arange(HALF)
    even = np.where(low % 2 == 0, low, ORDERS - 1 - low)
    twice = 2 * np.arange(QUARTER)[:, None] + 1
    heads, tails = [], []
    for order in (even, ORDERS - 1 - even):
        weight = np.where(order == 0, 1.0, 2.0)
        angle = (order[None, :] * twice % (2 * NLON)) * (math.pi / NLON)
        for wave in (weight * np.cos(angle), -weight * np.sin(angle)):
            head = wave.astype(ml_dtypes.bfloat16)
            heads.append(head)
            tails.append((wave - head.astype(np.float64)).astype(ml_dtypes.bfloat16))
    return np.stack(heads + tails)


def nn(a, b):
    return lax.dot_general(a, b, (((1,), (0,)), ((), ())), preferred_element_type=F32)


def nt(a, b):
    return lax.dot_general(a, b, (((1,), (1,)), ((), ())), preferred_element_type=F32)


def kernel(
    state, table, low_row, lows, diffusion, coupling, waves, out,
    wave_raw, wave_own, masked, st, cg, flat, s1, s2, r1, r2, s3, r3, s4, r4, mid, mid3, inv, send_x, recv_x, total,
    wave_sem, sem_cs, sem_cr, sem_1s, sem_1r, sem_2s, sem_2r, sem_3s, sem_3r, sem_4s, sem_4r, sem_us, sem_ur,
):
    slab = lax.axis_index("radial")
    mode = lax.axis_index("mode")
    far = mode // NEAR
    near = lax.rem(mode, NEAR)

    barrier = pltpu.get_barrier_semaphore()
    for k in range(1, SLABS):
        pl.semaphore_signal(barrier, inc=1, device_id=(lax.rem(slab + k, SLABS), mode), device_id_type=MESH)
    for k in range(1, NEAR):
        pl.semaphore_signal(barrier, inc=1, device_id=(slab, far * NEAR + lax.rem(near + k, NEAR)), device_id_type=MESH)
    for k in range(1, FAR):
        pl.semaphore_signal(barrier, inc=1, device_id=(slab, lax.rem(far + k, FAR) * NEAR + near), device_id_type=MESH)

    wave_copy = pltpu.make_async_copy(waves, wave_raw, wave_sem)
    wave_copy.start()

    st[...] = jnp.zeros_like(st)
    for f in range(3):
        for s in range(2):
            for c in range(2):
                for p in range(2):
                    row = f * 8 + s * 4 + c * 2 + p
                    st[row : row + 1, 0:ROWS] = state[p, f, s, c : c + 1, :]
    cg[slab] = st[...].astype(BF16)

    pl.semaphore_wait(barrier, SLABS + NEAR + FAR - 3)

    def x_copy(source, target, k, send, recv):
        return pltpu.make_async_remote_copy(
            src_ref=source, dst_ref=target, send_sem=send.at[k - 1], recv_sem=recv.at[k - 1],
            device_id=(lax.rem(slab + k, SLABS), mode), device_id_type=MESH,
        )

    def near_copy(source, target, k, send, recv):
        return pltpu.make_async_remote_copy(
            src_ref=source, dst_ref=target, send_sem=send.at[k - 1], recv_sem=recv.at[k - 1],
            device_id=(slab, far * NEAR + lax.rem(near + k, NEAR)), device_id_type=MESH,
        )

    def far_copy(source, target, k, send, recv):
        return pltpu.make_async_remote_copy(
            src_ref=source, dst_ref=target, send_sem=send.at[k - 1], recv_sem=recv.at[k - 1],
            device_id=(slab, lax.rem(far + k, FAR) * NEAR + near), device_id_type=MESH,
        )

    coefs = [x_copy(cg.at[slab], cg.at[slab], k, sem_cs, sem_cr) for k in range(1, SLABS)]
    for copy in coefs:
        copy.start()

    for p in range(2):
        low = lows[mode * 2 + p]
        low_even = lax.rem(low, 2) == 0
        for start, size in ((0, 512), (512, 128)):
            row = lax.broadcasted_iota(jnp.int32, (size, 128), 0) + start
            if start == 0:
                values = table[p, 0:512, :].astype(F32)
            else:
                last = table[p, 512:513, :].astype(F32)
                values = jnp.where(row == 512, jnp.broadcast_to(last, (128, 128)), 0.0)
            in_lower = row < ORDERS - low
            even_order = in_lower == low_even
            odd_sum = jnp.where(in_lower, lax.rem(row, 2), lax.rem(row + low, 2))
            sign = 1.0 - 2.0 * odd_sum.astype(F32)
            for q in range(2):
                north = jnp.where(even_order == (q == 0), values, 0.0)
                masked[p, start : start + size, q * 128 : (q + 1) * 128] = north.astype(BF16)
                masked[p, start : start + size, (2 + q) * 128 : (3 + q) * 128] = (north * sign).astype(BF16)

    for copy in coefs:
        copy.wait()

    gathered = [cg[i].astype(F32) for i in range(SLABS)]
    lhs = jnp.concatenate(
        [gathered[i][f * 8 : (f + 1) * 8] for f in range(3) for i in range(SLABS)], axis=0
    ).astype(BF16)
    first_pair = lax.rem(lax.broadcasted_iota(jnp.int32, (96, 512), 0), 2) == 0
    synth = jnp.where(first_pair, nn(lhs, masked[0]), nn(lhs, masked[1]))
    for b in range(4):
        flat[b * 96 : (b + 1) * 96, :] = synth[:, b * 128 : (b + 1) * 128]
    for g in range(3):
        block = flat[g * 128 : (g + 1) * 128, :].T
        s1[:, :, g * 128 : (g + 1) * 128] = block.reshape(NEAR, FAR, 128).astype(BF16)
    hop1 = [near_copy(s1.at[lax.rem(near + k, NEAR)], r1.at[near], k, sem_1s, sem_1r) for k in range(1, NEAR)]
    for copy in hop1:
        copy.start()
    r1[near] = s1[near]

    wave_copy.wait()
    pick = (
        lax.broadcasted_iota(jnp.int32, (HALF, HALF), 0) == jnp.broadcast_to(low_row[...], (HALF, HALF))
    ).astype(F32).astype(BF16)
    for q in range(8):
        wave_own[q] = nn(wave_raw[q], pick).astype(BF16)

    for copy in hop1:
        copy.wait()
    arrived = r1[...].reshape(128, QUARTER).astype(F32)
    for g in range(3):
        mid[g] = arrived[:, g * 128 : (g + 1) * 128]
    for z in range(FAR):
        s2[z] = jnp.concatenate([mid[g, pl.ds(z, NEAR, stride=FAR), :] for g in range(3)], axis=0).astype(BF16)
    hop2 = [far_copy(s2.at[lax.rem(far + k, FAR)], r2.at[far], k, sem_2s, sem_2r) for k in range(1, FAR)]
    for copy in hop2:
        copy.start()
    r2[far] = s2[far]

    row8 = lax.broadcasted_iota(jnp.int32, (8, PADDED), 0)
    lane8 = lax.broadcasted_iota(jnp.int32, (8, PADDED), 1)
    low8 = jnp.where(lax.rem(row8, 2) == 0, lows[mode * 2], lows[mode * 2 + 1])
    degree = jnp.where(lane8 < ORDERS - low8, low8 + lane8, lane8 - 1).astype(F32)
    degree = degree * (degree + 1.0) * (shell_step * shell_step)
    first_shell = row8 < 4
    for f in range(3):
        diagonal = []
        for s in range(8):
            radius = inner_radius + (s + 0.5) * shell_step
            diagonal.append(degree * (1.0 / (radius * radius)) + (1.0 / diffusion[f] + 2.0))
        leading = [jnp.ones((8, PADDED), F32), diagonal[0]]
        trailing = [jnp.ones((8, PADDED), F32), diagonal[7]]
        for s in range(1, 8):
            leading.append(diagonal[s] * leading[s] - leading[s - 1])
            trailing.append(diagonal[7 - s] * trailing[s] - trailing[s - 1])
        share = 1.0 / leading[8]
        scaled = [value * share for value in leading]

        def entry(i, j):
            return scaled[min(i, j)] * trailing[7 - max(i, j)]

        for i in range(SLABS):
            for j in range(i, SLABS):
                inv[f, 0, i, j] = jnp.where(first_shell, entry(2 * i, 2 * j), entry(2 * i + 1, 2 * j + 1))
                inv[f, 1, i, j] = jnp.where(first_shell, entry(2 * i, 2 * j + 1), entry(2 * i + 1, 2 * j))
                if i != j:
                    inv[f, 0, j, i] = jnp.where(first_shell, entry(2 * i, 2 * j), entry(2 * i + 1, 2 * j + 1))
                    inv[f, 1, j, i] = jnp.where(first_shell, entry(2 * i + 1, 2 * j), entry(2 * i, 2 * j + 1))

    for copy in hop2:
        copy.wait()
    arrived = r2[...].astype(F32)
    for g in range(3):
        flat[g * 128 : (g + 1) * 128, :] = arrived[:, g * 8 : (g + 1) * 8, :].reshape(128, 128).T

    parts = []
    for q in range(2):
        for c in range(2):
            rows = [
                jnp.concatenate(
                    [flat[pl.ds((h * 2 + q) * 96 + c * 2 + p, 24, stride=4), :] for p in range(2)], axis=1
                )
                for h in range(2)
            ]
            data = jnp.concatenate(rows, axis=0).astype(BF16)
            at = q * 2 + c
            parts.append(nt(data, wave_own[at]) + nt(data, wave_own[4 + at]))
    a, b = parts[0] + parts[2], parts[1] + parts[3]
    c, d = parts[0] - parts[2], parts[1] - parts[3]
    images = (a + b, a - b, c - d, c + d)
    sums = [[], [], [], []]
    for h in range(2):
        for left, right in ((0, 1), (0, 2), (1, 2)):
            u, v = h * 24 + left * 8, h * 24 + right * 8
            p1, p2, p3, p4 = [image[u : u + 8] * image[v : v + 8] for image in images]
            both, across = p1 + p2, p3 + p4
            turn, twist = p1 - p2, p4 - p3
            sums[0].append(both + across)
            sums[1].append(turn + twist)
            sums[2].append(both - across)
            sums[3].append(turn - twist)
    lowest = jnp.broadcast_to(low_row[...], (48, HALF)) == 0
    for q in range(2):
        for c in range(2):
            at = q * 2 + c
            value = jnp.concatenate(sums[at], axis=0)
            head = value.astype(BF16)
            tail = (value - head.astype(F32)).astype(BF16)
            answer = nn(head, wave_own[at]) + (nn(tail, wave_own[at]) + nn(head, wave_own[4 + at]))
            if q == 0:
                answer = answer * jnp.where(lowest, KAPPA, 0.5 * KAPPA)
            else:
                answer = answer * (0.5 * KAPPA)
            for h in range(2):
                for p in range(2):
                    flat[pl.ds((h * 2 + q) * 96 + c * 2 + p, 24, stride=4), :] = answer[
                        h * 24 : (h + 1) * 24, p * 128 : (p + 1) * 128
                    ]
    turned = [flat[g * 128 : (g + 1) * 128, :].T.reshape(FAR, NEAR, 128) for g in range(3)]
    s3[...] = jnp.concatenate(turned, axis=1).astype(BF16)
    hop3 = [far_copy(s3.at[lax.rem(far + k, FAR)], r3.at[far], k, sem_3s, sem_3r) for k in range(1, FAR)]
    for copy in hop3:
        copy.start()
    r3[far] = s3[far]
    for copy in hop3:
        copy.wait()
    mid3[...] = r3[...].astype(F32).reshape(FAR * 24, 128)
    for y in range(NEAR):
        s4[y] = jnp.concatenate(
            [mid3[pl.ds(g * 8 + y, FAR, stride=24), :] for g in range(3)], axis=1
        ).astype(BF16)
    hop4 = [near_copy(s4.at[lax.rem(near + k, NEAR)], r4.at[near], k, sem_4s, sem_4r) for k in range(1, NEAR)]
    for copy in hop4:
        copy.start()
    r4[near] = s4[near]
    for copy in hop4:
        copy.wait()

    arrived = r4[...].reshape(128, QUARTER).astype(F32)
    for g in range(3):
        flat[g * 128 : (g + 1) * 128, :] = arrived[:, g * 128 : (g + 1) * 128].T
    lhs = jnp.concatenate([flat[b * 96 : (b + 1) * 96, :] for b in range(4)], axis=1).astype(BF16)
    first_pair = lax.rem(lax.broadcasted_iota(jnp.int32, (96, PADDED), 0), 2) == 0
    nonlinear = jnp.where(first_pair, nt(lhs, masked[0]), nt(lhs, masked[1]))
    for f in range(3):
        own = st[f * 8 : (f + 1) * 8, :] * (2.0 / diffusion[f])
        drives, swapped = [], []
        for i in range(SLABS):
            start = f * 32 + i * 8
            mine = (slab == i).astype(F32)
            drive = nonlinear[start : start + 8] * coupling[f] + own * mine
            drives.append(drive)
            swapped.append(pltpu.roll(drive, 4, 0))
        for i in range(SLABS):
            value = inv[f, 0, i, 0] * drives[0] + inv[f, 1, i, 0] * swapped[0]
            for j in range(1, SLABS):
                value = value + inv[f, 0, i, j] * drives[j] + inv[f, 1, i, j] * swapped[j]
            send_x[i, f * 8 : (f + 1) * 8, :] = value
    last = [x_copy(send_x.at[lax.rem(slab + k, SLABS)], recv_x.at[k - 1], k, sem_us, sem_ur) for k in range(1, SLABS)]
    for copy in last:
        copy.start()
    total[...] = send_x[slab] - st[...]
    for copy in last:
        copy.wait()
    total[...] = total[...] + recv_x[0] + recv_x[1] + recv_x[2]
    for f in range(3):
        for s in range(2):
            for c in range(2):
                for p in range(2):
                    row = f * 8 + s * 4 + c * 2 + p
                    out[p, f, s, c : c + 1, :] = total[row : row + 1, 0:ROWS]


def body(spectral_state, synthesis_table, low_orders, diffusion, coupling):
    low_row = low_orders.reshape(HALF // 2, 2).T.reshape(1, HALF)
    vmem = pl.BlockSpec(memory_space=pltpu.VMEM)
    smem = pl.BlockSpec(memory_space=pltpu.SMEM)
    dma = pltpu.SemaphoreType.DMA
    return pl.pallas_call(
        kernel,
        out_shape=jax.ShapeDtypeStruct(spectral_state.shape, F32),
        in_specs=[vmem, vmem, vmem, smem, smem, smem, pl.BlockSpec(memory_space=pl.ANY)],
        out_specs=vmem,
        scratch_shapes=[
            pltpu.VMEM((8, QUARTER, HALF), BF16),
            pltpu.VMEM((8, QUARTER, HALF), BF16),
            pltpu.VMEM((2, PADDED, 512), BF16),
            pltpu.VMEM((24, PADDED), F32),
            pltpu.VMEM((SLABS, 24, PADDED), BF16),
            pltpu.VMEM((384, 128), F32),
            pltpu.VMEM((NEAR, FAR, 384), BF16),
            pltpu.VMEM((FAR, 24, 128), BF16),
            pltpu.VMEM((NEAR, FAR, 384), BF16),
            pltpu.VMEM((FAR, 24, 128), BF16),
            pltpu.VMEM((FAR, 24, 128), BF16),
            pltpu.VMEM((FAR, 24, 128), BF16),
            pltpu.VMEM((NEAR, FAR, 384), BF16),
            pltpu.VMEM((NEAR, FAR, 384), BF16),
            pltpu.VMEM((3, 128, 128), F32),
            pltpu.VMEM((FAR * 24, 128), F32),
            pltpu.VMEM((3, 2, SLABS, SLABS, 8, PADDED), F32),
            pltpu.VMEM((SLABS, 24, PADDED), F32),
            pltpu.VMEM((SLABS - 1, 24, PADDED), F32),
            pltpu.VMEM((24, PADDED), F32),
            dma,
            dma((SLABS - 1,)), dma((SLABS - 1,)),
            dma((NEAR - 1,)), dma((NEAR - 1,)),
            dma((FAR - 1,)), dma((FAR - 1,)),
            dma((FAR - 1,)), dma((FAR - 1,)),
            dma((NEAR - 1,)), dma((NEAR - 1,)),
            dma((SLABS - 1,)), dma((SLABS - 1,)),
        ],
        compiler_params=pltpu.CompilerParams(
            collective_id=0, has_side_effects=True, vmem_limit_bytes=40 * 1024 * 1024
        ),
    )(spectral_state, synthesis_table, low_row, low_orders, diffusion, coupling, jnp.asarray(wave_tables()))


def solution(mesh):
    placed = (P("mode", None, "radial", None, None), P("mode", None, "radial"), P(), P(), P())
    return jax.shard_map(
        body,
        mesh=mesh,
        in_specs=placed,
        out_specs=P("mode", None, "radial", None, None),
        check_vma=False,
    )
```

profile of v0, /device:TPU:1, one launch (start us, length us, event | category | flops | bytes accessed | tf_op | source)
XLA Modules:
  0.0 63.4 jit_solution(13720276992772162894)
XLA Ops:
  0.0 0.8 %reshape.6 = s32[128,2]{1,0:T(8,128)S(1)} reshape(s32[256]{0:T(256)} %lows.1) | data formatting | bytes 2048 | tf_op jit(solution)/shard_map/reshape | solution.py:300
  0.8 0.1 copy.8
  0.9 1.0 %copy.9.table = bf16[2,513,128]{2,1,0:T(8,128)(2,1)S(1)} copy(bf16[2,513,128]{2,0,1:T(2,128)(2,1)} %param.7) | data formatting | bytes 525312 | tf_op args[1]
  1.9 0.0 copy-start
  1.9 1.4 %copy-done = bf16[8,384,256]{2,1,0:T(8,128)(2,1)S(1)} copy-done((bf16[8,384,256]{2,1,0:T(8,128)(2,1)S(1)}, bf16[8,384,256]{2,1,0:T(8,128)(2,1)}, u32[]{:S(2)}) %copy-start) | copy-done | bytes 1572888
  3.3 0.0 copy-start.1
  3.3 0.8 %copy-done.1 = f32[2,3,2,2,513]{4,3,2,1,0:T(2,128)S(1)} copy-done((f32[2,3,2,2,513]{4,3,2,1,0:T(2,128)S(1)}, f32[2,3,2,2,513]{4,3,2,1,0:T(2,128)}, u32[]{:S(2)}) %copy-start.1) | copy-done | bytes 49272
  4.1 0.0 copy-start.2
  4.1 0.7 %copy-done.2 = s32[256]{0:T(256)S(1)} copy-done((s32[256]{0:T(256)S(1)}, s32[256]{0:T(256)}, u32[]{:S(2)}) %copy-start.2) | copy-done | bytes 1048
  4.8 0.0 copy-start.3
  4.8 0.7 %copy-done.3 = f32[3]{0:T(128)S(1)} copy-done((f32[3]{0:T(128)S(1)}, f32[3]{0:T(128)}, u32[]{:S(2)}) %copy-start.3) | copy-done | bytes 36
  5.5 0.0 copy-start.4
  5.5 0.7 %copy-done.4 = f32[3]{0:T(128)S(1)} copy-done((f32[3]{0:T(128)S(1)}, f32[3]{0:T(128)}, u32[]{:S(2)}) %copy-start.4) | copy-done | bytes 36
  6.1 56.7 %shard_map.64 = f32[2,3,2,2,513]{4,3,2,1,0:T(2,128)S(1)} custom-call(f32[2,3,2,2,513]{4,3,2,1,0:T(2,128)S(1)} %copy-done.1, bf16[2,513,128]{2,1,0:T(8,128)(2,1)S(1)} %copy.9.table, s32[1,256]{1,0:T(1,128)S(1)} %bitcast.2, s32[256]{0:T(256)S(1)} %copy-done.2, f32[3]{0:T(128)S(1)} %copy-done.3, f32[3]{0:T(128)S(1)} %copy-done.4, bf16[8,384,256]{2,1,0:T(8,128)(2,1)S(1)} %copy-done), custom_call_target="tpu_custom_call" | custom-call | tf_op jit(solution)/shard_map/pallas_call | solution.py:304
  62.8 0.6 copy.11
Async XLA Ops:
  1.9 1.4 %copy-start = (bf16[8,384,256]{2,1,0:T(8,128)(2,1)S(1)}, bf16[8,384,256]{2,1,0:T(8,128)(2,1)}, u32[]{:S(2)}) copy-start(bf16[8,384,256]{2,1,0:T(8,128)(2,1)} %constant.2.clone.waves) | copy-start | bytes 4718596
  3.3 0.8 %copy-start.1 = (f32[2,3,2,2,513]{4,3,2,1,0:T(2,128)S(1)}, f32[2,3,2,2,513]{4,3,2,1,0:T(2,128)}, u32[]{:S(2)}) copy-start(f32[2,3,2,2,513]{4,3,2,1,0:T(2,128)} %state.1) | copy-start | bytes 147748
  4.1 0.7 %copy-start.2 = (s32[256]{0:T(256)S(1)}, s32[256]{0:T(256)}, u32[]{:S(2)}) copy-start(s32[256]{0:T(256)} %lows.1) | copy-start | bytes 3076
  4.8 0.7 %copy-start.3 = (f32[3]{0:T(128)S(1)}, f32[3]{0:T(128)}, u32[]{:S(2)}) copy-start(f32[3]{0:T(128)} %diffusion.1) | copy-start | bytes 40
  5.5 0.7 %copy-start.4 = (f32[3]{0:T(128)S(1)}, f32[3]{0:T(128)}, u32[]{:S(2)}) copy-start(f32[3]{0:T(128)} %coupling.1) | copy-start | bytes 40
where the time goes:
time: 63.7 us; the launch traced here: 63.4 us
  Pallas kernels  56.7 us (89%)
  local copies, waits for them, and re-layouts  6.73 us (11%)
    pallas_call x1, Pallas kernels, body(): pl.pallas_call(kernel, out_shape=jax.ShapeDtypeStruct(spectral_state.shap...  56.7 us
    unnamed x12, local copies, waits for them, and re-layouts  5.86 us

commit v1 on v0

--- a/solution.py
+++ b/solution.py
@@ -22,6 +22,9 @@
 SLABS = 4
 NEAR = 8
 FAR = 16
+X_STEPS = (2, 1, 3)
+NEAR_STEPS = ((2, 0), (2, 1), (1, 0), (3, 0), (1, 1), (3, 1), (0, 1))
+FAR_STEPS = (8, 7, 9, 6, 10, 5, 11, 4, 12, 3, 13, 2, 14, 1, 15)
 KAPPA = 2.0 * math.sqrt(ORDERS * (ORDERS + 1) / (NLAT * NLON))
 MESH = pl.DeviceIdType.MESH
 F32 = jnp.float32
@@ -52,27 +55,48 @@
 
 
 def kernel(
-    state, table, low_row, lows, diffusion, coupling, waves, out,
+    state_hbm, table_hbm, low_hbm, lows_hbm, diffusion_hbm, coupling_hbm, waves, out,
+    state, table, low_row, lows, diffusion, coupling,
     wave_raw, wave_own, masked, st, cg, flat, s1, s2, r1, r2, s3, r3, s4, r4, mid, mid3, inv, send_x, recv_x, total,
-    wave_sem, sem_cs, sem_cr, sem_1s, sem_1r, sem_2s, sem_2r, sem_3s, sem_3r, sem_4s, sem_4r, sem_us, sem_ur,
+    load_sem, sem_cs, sem_cr, sem_1s, sem_1r, sem_2s, sem_2r, sem_3s, sem_3r, sem_4s, sem_4r, sem_us, sem_ur,
 ):
     slab = lax.axis_index("radial")
     mode = lax.axis_index("mode")
     far = mode // NEAR
     near = lax.rem(mode, NEAR)
 
+    def x_peer(step):
+        return lax.rem(slab + step, SLABS)
+
+    def near_peer(step):
+        return lax.rem(near // 2 + step[0], 4) * 2 + lax.rem(lax.rem(near, 2) + step[1], 2)
+
+    def far_peer(step):
+        return lax.rem(far + step, FAR)
+
     barrier = pltpu.get_barrier_semaphore()
-    for k in range(1, SLABS):
-        pl.semaphore_signal(barrier, inc=1, device_id=(lax.rem(slab + k, SLABS), mode), device_id_type=MESH)
-    for k in range(1, NEAR):
-        pl.semaphore_signal(barrier, inc=1, device_id=(slab, far * NEAR + lax.rem(near + k, NEAR)), device_id_type=MESH)
-    for k in range(1, FAR):
-        pl.semaphore_signal(barrier, inc=1, device_id=(slab, lax.rem(far + k, FAR) * NEAR + near), device_id_type=MESH)
-
-    wave_copy = pltpu.make_async_copy(waves, wave_raw, wave_sem)
-    wave_copy.start()
+    for step in FAR_STEPS:
+        pl.semaphore_signal(barrier, inc=1, device_id=(slab, far_peer(step) * NEAR + near), device_id_type=MESH)
+    for step in NEAR_STEPS:
+        pl.semaphore_signal(barrier, inc=1, device_id=(slab, far * NEAR + near_peer(step)), device_id_type=MESH)
+    for step in X_STEPS:
+        pl.semaphore_signal(barrier, inc=1, device_id=(x_peer(step), mode), device_id_type=MESH)
+
+    loads = [
+        pltpu.make_async_copy(source, target, load_sem.at[i])
+        for i, (source, target) in enumerate(
+            (
+                (lows_hbm, lows), (diffusion_hbm, diffusion), (coupling_hbm, coupling), (state_hbm, state),
+                (table_hbm, table), (low_hbm, low_row), (waves, wave_raw),
+            )
+        )
+    ]
+    for load in loads:
+        load.start()
 
     st[...] = jnp.zeros_like(st)
+    for load in loads[:4]:
+        load.wait()
     for f in range(3):
         for s in range(2):
             for c in range(2):
@@ -81,30 +105,31 @@
                     st[row : row + 1, 0:ROWS] = state[p, f, s, c : c + 1, :]
     cg[slab] = st[...].astype(BF16)
 
-    pl.semaphore_wait(barrier, SLABS + NEAR + FAR - 3)
-
-    def x_copy(source, target, k, send, recv):
+    def x_copy(source, target, i, send, recv):
         return pltpu.make_async_remote_copy(
-            src_ref=source, dst_ref=target, send_sem=send.at[k - 1], recv_sem=recv.at[k - 1],
-            device_id=(lax.rem(slab + k, SLABS), mode), device_id_type=MESH,
+            src_ref=source, dst_ref=target, send_sem=send.at[i], recv_sem=recv.at[i],
+            device_id=(x_peer(X_STEPS[i]), mode), device_id_type=MESH,
         )
 
-    def near_copy(source, target, k, send, recv):
-        return pltpu.make_async_remote_copy(
-            src_ref=source, dst_ref=target, send_sem=send.at[k - 1], recv_sem=recv.at[k - 1],
-            device_id=(slab, far * NEAR + lax.rem(near + k, NEAR)), device_id_type=MESH,
-        )
-
-    def far_copy(source, target, k, send, recv):
-        return pltpu.make_async_remote_copy(
-            src_ref=source, dst_ref=target, send_sem=send.at[k - 1], recv_sem=recv.at[k - 1],
-            device_id=(slab, lax.rem(far + k, FAR) * NEAR + near), device_id_type=MESH,
-        )
-
-    coefs = [x_copy(cg.at[slab], cg.at[slab], k, sem_cs, sem_cr) for k in range(1, SLABS)]
-    for copy in coefs:
-        copy.start()
-
+    def near_copies(source, target, send, recv):
+        return [
+            pltpu.make_async_remote_copy(
+                src_ref=source.at[near_peer(step)], dst_ref=target.at[near], send_sem=send.at[i], recv_sem=recv.at[i],
+                device_id=(slab, far * NEAR + near_peer(step)), device_id_type=MESH,
+            )
+            for i, step in enumerate(NEAR_STEPS)
+        ]
+
+    def far_copies(source, target, send, recv):
+        return [
+            pltpu.make_async_remote_copy(
+                src_ref=source.at[far_peer(step)], dst_ref=target.at[far], send_sem=send.at[i], recv_sem=recv.at[i],
+                device_id=(slab, far_peer(step) * NEAR + near), device_id_type=MESH,
+            )
+            for i, step in enumerate(FAR_STEPS)
+        ]
+
+    loads[4].wait()
     for p in range(2):
         low = lows[mode * 2 + p]
         low_even = lax.rem(low, 2) == 0
@@ -124,43 +149,16 @@
                 masked[p, start : start + size, q * 128 : (q + 1) * 128] = north.astype(BF16)
                 masked[p, start : start + size, (2 + q) * 128 : (3 + q) * 128] = (north * sign).astype(BF16)
 
-    for copy in coefs:
-        copy.wait()
-
-    gathered = [cg[i].astype(F32) for i in range(SLABS)]
-    lhs = jnp.concatenate(
-        [gathered[i][f * 8 : (f + 1) * 8] for f in range(3) for i in range(SLABS)], axis=0
-    ).astype(BF16)
-    first_pair = lax.rem(lax.broadcasted_iota(jnp.int32, (96, 512), 0), 2) == 0
-    synth = jnp.where(first_pair, nn(lhs, masked[0]), nn(lhs, masked[1]))
-    for b in range(4):
-        flat[b * 96 : (b + 1) * 96, :] = synth[:, b * 128 : (b + 1) * 128]
-    for g in range(3):
-        block = flat[g * 128 : (g + 1) * 128, :].T
-        s1[:, :, g * 128 : (g + 1) * 128] = block.reshape(NEAR, FAR, 128).astype(BF16)
-    hop1 = [near_copy(s1.at[lax.rem(near + k, NEAR)], r1.at[near], k, sem_1s, sem_1r) for k in range(1, NEAR)]
-    for copy in hop1:
-        copy.start()
-    r1[near] = s1[near]
-
-    wave_copy.wait()
-    pick = (
-        lax.broadcasted_iota(jnp.int32, (HALF, HALF), 0) == jnp.broadcast_to(low_row[...], (HALF, HALF))
-    ).astype(F32).astype(BF16)
+    for load in loads[5:]:
+        load.wait()
+    down = lax.broadcasted_iota(jnp.int32, (HALF, HALF), 0)
+    across = lax.broadcasted_iota(jnp.int32, (HALF, HALF), 1)
+    regroup = (down == lax.rem(across, 128) * 2 + across // 128).astype(F32).astype(BF16)
+    natural = jnp.broadcast_to(low_row[...], (HALF, HALF))
+    pick = nn((down == natural).astype(F32).astype(BF16), regroup).astype(BF16)
+    lowest = pick[0:1, :].astype(F32)
     for q in range(8):
         wave_own[q] = nn(wave_raw[q], pick).astype(BF16)
-
-    for copy in hop1:
-        copy.wait()
-    arrived = r1[...].reshape(128, QUARTER).astype(F32)
-    for g in range(3):
-        mid[g] = arrived[:, g * 128 : (g + 1) * 128]
-    for z in range(FAR):
-        s2[z] = jnp.concatenate([mid[g, pl.ds(z, NEAR, stride=FAR), :] for g in range(3)], axis=0).astype(BF16)
-    hop2 = [far_copy(s2.at[lax.rem(far + k, FAR)], r2.at[far], k, sem_2s, sem_2r) for k in range(1, FAR)]
-    for copy in hop2:
-        copy.start()
-    r2[far] = s2[far]
 
     row8 = lax.broadcasted_iota(jnp.int32, (8, PADDED), 0)
     lane8 = lax.broadcasted_iota(jnp.int32, (8, PADDED), 1)
@@ -191,6 +189,43 @@
                 if i != j:
                     inv[f, 0, j, i] = jnp.where(first_shell, entry(2 * i, 2 * j), entry(2 * i + 1, 2 * j + 1))
                     inv[f, 1, j, i] = jnp.where(first_shell, entry(2 * i + 1, 2 * j), entry(2 * i, 2 * j + 1))
+
+    pl.semaphore_wait(barrier, SLABS + NEAR + FAR - 3)
+
+    coefs = [x_copy(cg.at[slab], cg.at[slab], i, sem_cs, sem_cr) for i in range(SLABS - 1)]
+    for copy in coefs:
+        copy.start()
+
+    for copy in coefs:
+        copy.wait()
+
+    gathered = [cg[i].astype(F32) for i in range(SLABS)]
+    lhs = jnp.concatenate(
+        [gathered[i][f * 8 : (f + 1) * 8] for f in range(3) for i in range(SLABS)], axis=0
+    ).astype(BF16)
+    first_pair = lax.rem(lax.broadcasted_iota(jnp.int32, (96, 512), 0), 2) == 0
+    synth = jnp.where(first_pair, nn(lhs, masked[0]), nn(lhs, masked[1]))
+    for b in range(4):
+        flat[b * 96 : (b + 1) * 96, :] = synth[:, b * 128 : (b + 1) * 128]
+    for g in range(3):
+        block = flat[g * 128 : (g + 1) * 128, :].T
+        s1[:, :, g * 128 : (g + 1) * 128] = block.reshape(NEAR, FAR, 128).astype(BF16)
+    hop1 = near_copies(s1, r1, sem_1s, sem_1r)
+    for copy in hop1:
+        copy.start()
+    r1[near] = s1[near]
+
+    for copy in hop1:
+        copy.wait()
+    arrived = r1[...].reshape(128, QUARTER).astype(F32)
+    for g in range(3):
+        mid[g] = arrived[:, g * 128 : (g + 1) * 128]
+    for z in range(FAR):
+        s2[z] = jnp.concatenate([mid[g, pl.ds(z, NEAR, stride=FAR), :] for g in range(3)], axis=0).astype(BF16)
+    hop2 = far_copies(s2, r2, sem_2s, sem_2r)
+    for copy in hop2:
+        copy.start()
+    r2[far] = s2[far]
 
     for copy in hop2:
         copy.wait()
@@ -224,7 +259,6 @@
             sums[1].append(turn + twist)
             sums[2].append(both - across)
             sums[3].append(turn - twist)
-    lowest = jnp.broadcast_to(low_row[...], (48, HALF)) == 0
     for q in range(2):
         for c in range(2):
             at = q * 2 + c
@@ -233,7 +267,7 @@
             tail = (value - head.astype(F32)).astype(BF16)
             answer = nn(head, wave_own[at]) + (nn(tail, wave_own[at]) + nn(head, wave_own[4 + at]))
             if q == 0:
-                answer = answer * jnp.where(lowest, KAPPA, 0.5 * KAPPA)
+                answer = answer * (0.5 * KAPPA * (1.0 + lowest))
             else:
                 answer = answer * (0.5 * KAPPA)
             for h in range(2):
@@ -243,7 +277,7 @@
                     ]
     turned = [flat[g * 128 : (g + 1) * 128, :].T.reshape(FAR, NEAR, 128) for g in range(3)]
     s3[...] = jnp.concatenate(turned, axis=1).astype(BF16)
-    hop3 = [far_copy(s3.at[lax.rem(far + k, FAR)], r3.at[far], k, sem_3s, sem_3r) for k in range(1, FAR)]
+    hop3 = far_copies(s3, r3, sem_3s, sem_3r)
     for copy in hop3:
         copy.start()
     r3[far] = s3[far]
@@ -254,7 +288,7 @@
         s4[y] = jnp.concatenate(
             [mid3[pl.ds(g * 8 + y, FAR, stride=24), :] for g in range(3)], axis=1
         ).astype(BF16)
-    hop4 = [near_copy(s4.at[lax.rem(near + k, NEAR)], r4.at[near], k, sem_4s, sem_4r) for k in range(1, NEAR)]
+    hop4 = near_copies(s4, r4, sem_4s, sem_4r)
     for copy in hop4:
         copy.start()
     r4[near] = s4[near]
@@ -281,7 +315,7 @@
             for j in range(1, SLABS):
                 value = value + inv[f, 0, i, j] * drives[j] + inv[f, 1, i, j] * swapped[j]
             send_x[i, f * 8 : (f + 1) * 8, :] = value
-    last = [x_copy(send_x.at[lax.rem(slab + k, SLABS)], recv_x.at[k - 1], k, sem_us, sem_ur) for k in range(1, SLABS)]
+    last = [x_copy(send_x.at[x_peer(X_STEPS[i])], recv_x.at[i], i, sem_us, sem_ur) for i in range(SLABS - 1)]
     for copy in last:
         copy.start()
     total[...] = send_x[slab] - st[...]
@@ -297,16 +331,22 @@
 
 
 def body(spectral_state, synthesis_table, low_orders, diffusion, coupling):
-    low_row = low_orders.reshape(HALF // 2, 2).T.reshape(1, HALF)
+    low_row = low_orders.reshape(1, HALF)
     vmem = pl.BlockSpec(memory_space=pltpu.VMEM)
-    smem = pl.BlockSpec(memory_space=pltpu.SMEM)
+    hbm = pl.BlockSpec(memory_space=pltpu.HBM)
     dma = pltpu.SemaphoreType.DMA
     return pl.pallas_call(
         kernel,
         out_shape=jax.ShapeDtypeStruct(spectral_state.shape, F32),
-        in_specs=[vmem, vmem, vmem, smem, smem, smem, pl.BlockSpec(memory_space=pl.ANY)],
+        in_specs=[hbm] * 7,
         out_specs=vmem,
         scratch_shapes=[
+            pltpu.VMEM(spectral_state.shape, F32),
+            pltpu.VMEM(synthesis_table.shape, BF16),
+            pltpu.VMEM((1, HALF), jnp.int32),
+            pltpu.SMEM((HALF,), jnp.int32),
+            pltpu.SMEM((3,), F32),
+            pltpu.SMEM((3,), F32),
             pltpu.VMEM((8, QUARTER, HALF), BF16),
             pltpu.VMEM((8, QUARTER, HALF), BF16),
             pltpu.VMEM((2, PADDED, 512), BF16),
@@ -327,7 +367,7 @@
             pltpu.VMEM((SLABS, 24, PADDED), F32),
             pltpu.VMEM((SLABS - 1, 24, PADDED), F32),
             pltpu.VMEM((24, PADDED), F32),
-            dma,
+            dma((7,)),
             dma((SLABS - 1,)), dma((SLABS - 1,)),
             dma((NEAR - 1,)), dma((NEAR - 1,)),
             dma((FAR - 1,)), dma((FAR - 1,)),
@@ -336,7 +376,7 @@
             dma((SLABS - 1,)), dma((SLABS - 1,)),
         ],
         compiler_params=pltpu.CompilerParams(
-            collective_id=0, has_side_effects=True, vmem_limit_bytes=40 * 1024 * 1024
+            collective_id=0, has_side_effects=True, vmem_limit_bytes=63 * 1024 * 1024
         ),
     )(spectral_state, synthesis_table, low_row, low_orders, diffusion, coupling, jnp.asarray(wave_tables()))
 

time: 63.7 us -> 55.3 us (0.87)
  Pallas kernels: 56.7 us -> 51.9 us
  local copies, waits for them, and re-layouts: 6.73 us -> 3.15 us
    pallas_call x1, Pallas kernels: 56.7 us -> 51.9 us  [body(): pl.pallas_call(kernel, out_shape=jax.ShapeDtypeStruct(spectral_state.shap...]
    unnamed x12 -> x2, local copies, waits for them, and re-layouts: 5.86 us -> 3.15 us
    reshape x1 -> x0, local copies, waits for them, and re-layouts: 0.81 us -> none  [body(): low_row = low_orders.reshape(HALF // 2, 2).T.reshape(1, HALF)]
where the time goes in v1:
time: 55.3 us; the launch traced here: 55.1 us
  Pallas kernels  51.9 us (94%)
  local copies, waits for them, and re-layouts  3.15 us (6%)
    pallas_call x1, Pallas kernels, body(): pl.pallas_call(kernel, out_shape=jax.ShapeDtypeStruct(spectral_state.shap...  51.9 us
    unnamed x2, local copies, waits for them, and re-layouts  3.15 us

profile of v1, /device:TPU:1, one launch (start us, length us, event | category | flops | bytes accessed | tf_op | source)
XLA Modules:
  0.0 55.1 jit_solution(6925801918993994885)
XLA Ops:
  0.0 1.7 %copy.7.table_hbm = bf16[2,513,128]{2,1,0:T(8,128)(2,1)} copy(bf16[2,513,128]{2,0,1:T(2,128)(2,1)} %param.7) | data formatting | bytes 525312 | tf_op args[1]
  1.7 51.9 %shard_map.64 = f32[2,3,2,2,513]{4,3,2,1,0:T(2,128)} custom-call(f32[2,3,2,2,513]{4,3,2,1,0:T(2,128)} %state_hbm.1, bf16[2,513,128]{2,1,0:T(8,128)(2,1)} %copy.7.table_hbm, s32[1,256]{1,0:T(1,128)} %bitcast.1, s32[256]{0:T(256)} %lows_hbm.1, f32[3]{0:T(128)} %diffusion_hbm.1, f32[3]{0:T(128)} %coupling_hbm.1, bf16[8,384,256]{2,1,0:T(8,128)(2,1)} %constant.2.clone.waves), custom_call_target="tpu_custom_call" | custom-call | tf_op jit(solution)/shard_map/pallas_call | solution.py:338
  53.6 1.5 %copy.9 = f32[2,3,2,2,513]{4,3,2,1,0:T(2,128)} copy(f32[2,3,2,2,513]{4,3,2,1,0:T(2,128)} %shard_map.64) | data formatting | bytes 98496

commit v2 on v1

--- a/solution.py
+++ b/solution.py
@@ -25,6 +25,7 @@
 X_STEPS = (2, 1, 3)
 NEAR_STEPS = ((2, 0), (2, 1), (1, 0), (3, 0), (1, 1), (3, 1), (0, 1))
 FAR_STEPS = (8, 7, 9, 6, 10, 5, 11, 4, 12, 3, 13, 2, 14, 1, 15)
+GREETED = (2, 14, 1, 15)
 KAPPA = 2.0 * math.sqrt(ORDERS * (ORDERS + 1) / (NLAT * NLON))
 MESH = pl.DeviceIdType.MESH
 F32 = jnp.float32
@@ -58,7 +59,7 @@
     state_hbm, table_hbm, low_hbm, lows_hbm, diffusion_hbm, coupling_hbm, waves, out,
     state, table, low_row, lows, diffusion, coupling,
     wave_raw, wave_own, masked, st, cg, flat, s1, s2, r1, r2, s3, r3, s4, r4, mid, mid3, inv, send_x, recv_x, total,
-    load_sem, sem_cs, sem_cr, sem_1s, sem_1r, sem_2s, sem_2r, sem_3s, sem_3r, sem_4s, sem_4r, sem_us, sem_ur,
+    relay, load_sem, sem_cs, sem_cr, sem_1s, sem_1r, sem_2s, sem_2r, sem_3s, sem_3r, sem_4s, sem_4r, sem_us, sem_ur,
 ):
     slab = lax.axis_index("radial")
     mode = lax.axis_index("mode")
@@ -75,7 +76,7 @@
         return lax.rem(far + step, FAR)
 
     barrier = pltpu.get_barrier_semaphore()
-    for step in FAR_STEPS:
+    for step in GREETED:
         pl.semaphore_signal(barrier, inc=1, device_id=(slab, far_peer(step) * NEAR + near), device_id_type=MESH)
     for step in NEAR_STEPS:
         pl.semaphore_signal(barrier, inc=1, device_id=(slab, far * NEAR + near_peer(step)), device_id_type=MESH)
@@ -149,6 +150,18 @@
                 masked[p, start : start + size, q * 128 : (q + 1) * 128] = north.astype(BF16)
                 masked[p, start : start + size, (2 + q) * 128 : (3 + q) * 128] = (north * sign).astype(BF16)
 
+    pl.semaphore_wait(barrier, SLABS - 1 + NEAR - 1 + len(GREETED))
+
+    coefs = [x_copy(cg.at[slab], cg.at[slab], i, sem_cs, sem_cr) for i in range(SLABS - 1)]
+    for copy in coefs:
+        copy.start()
+
+    def pass_on(i, reach):
+        for step in (reach, FAR - reach):
+            pl.semaphore_signal(relay.at[i], inc=1, device_id=(slab, far_peer(step) * NEAR + near), device_id_type=MESH)
+
+    pass_on(0, 2)
+
     for load in loads[5:]:
         load.wait()
     down = lax.broadcasted_iota(jnp.int32, (HALF, HALF), 0)
@@ -159,6 +172,28 @@
     lowest = pick[0:1, :].astype(F32)
     for q in range(8):
         wave_own[q] = nn(wave_raw[q], pick).astype(BF16)
+
+    pl.semaphore_wait(relay.at[0], 2)
+    pass_on(1, 4)
+
+    for copy in coefs:
+        copy.wait()
+
+    gathered = [cg[i].astype(F32) for i in range(SLABS)]
+    lhs = jnp.concatenate(
+        [gathered[i][f * 8 : (f + 1) * 8] for f in range(3) for i in range(SLABS)], axis=0
+    ).astype(BF16)
+    first_pair = lax.rem(lax.broadcasted_iota(jnp.int32, (96, 512), 0), 2) == 0
+    synth = jnp.where(first_pair, nn(lhs, masked[0]), nn(lhs, masked[1]))
+    for b in range(4):
+        flat[b * 96 : (b + 1) * 96, :] = synth[:, b * 128 : (b + 1) * 128]
+    for g in range(3):
+        block = flat[g * 128 : (g + 1) * 128, :].T
+        s1[:, :, g * 128 : (g + 1) * 128] = block.reshape(NEAR, FAR, 128).astype(BF16)
+    hop1 = near_copies(s1, r1, sem_1s, sem_1r)
+    for copy in hop1:
+        copy.start()
+    r1[near] = s1[near]
 
     row8 = lax.broadcasted_iota(jnp.int32, (8, PADDED), 0)
     lane8 = lax.broadcasted_iota(jnp.int32, (8, PADDED), 1)
@@ -190,30 +225,6 @@
                     inv[f, 0, j, i] = jnp.where(first_shell, entry(2 * i, 2 * j), entry(2 * i + 1, 2 * j + 1))
                     inv[f, 1, j, i] = jnp.where(first_shell, entry(2 * i + 1, 2 * j), entry(2 * i, 2 * j + 1))
 
-    pl.semaphore_wait(barrier, SLABS + NEAR + FAR - 3)
-
-    coefs = [x_copy(cg.at[slab], cg.at[slab], i, sem_cs, sem_cr) for i in range(SLABS - 1)]
-    for copy in coefs:
-        copy.start()
-
-    for copy in coefs:
-        copy.wait()
-
-    gathered = [cg[i].astype(F32) for i in range(SLABS)]
-    lhs = jnp.concatenate(
-        [gathered[i][f * 8 : (f + 1) * 8] for f in range(3) for i in range(SLABS)], axis=0
-    ).astype(BF16)
-    first_pair = lax.rem(lax.broadcasted_iota(jnp.int32, (96, 512), 0), 2) == 0
-    synth = jnp.where(first_pair, nn(lhs, masked[0]), nn(lhs, masked[1]))
-    for b in range(4):
-        flat[b * 96 : (b + 1) * 96, :] = synth[:, b * 128 : (b + 1) * 128]
-    for g in range(3):
-        block = flat[g * 128 : (g + 1) * 128, :].T
-        s1[:, :, g * 128 : (g + 1) * 128] = block.reshape(NEAR, FAR, 128).astype(BF16)
-    hop1 = near_copies(s1, r1, sem_1s, sem_1r)
-    for copy in hop1:
-        copy.start()
-    r1[near] = s1[near]
 
     for copy in hop1:
         copy.wait()
@@ -222,6 +233,7 @@
         mid[g] = arrived[:, g * 128 : (g + 1) * 128]
     for z in range(FAR):
         s2[z] = jnp.concatenate([mid[g, pl.ds(z, NEAR, stride=FAR), :] for g in range(3)], axis=0).astype(BF16)
+    pl.semaphore_wait(relay.at[1], 2)
     hop2 = far_copies(s2, r2, sem_2s, sem_2r)
     for copy in hop2:
         copy.start()
@@ -367,6 +379,7 @@
             pltpu.VMEM((SLABS, 24, PADDED), F32),
             pltpu.VMEM((SLABS - 1, 24, PADDED), F32),
             pltpu.VMEM((24, PADDED), F32),
+            pltpu.SemaphoreType.REGULAR((2,)),
             dma((7,)),
             dma((SLABS - 1,)), dma((SLABS - 1,)),
             dma((NEAR - 1,)), dma((NEAR - 1,)),

time: 55.3 us -> 52.1 us (0.942)
  Pallas kernels: 51.9 us -> 48.8 us
    pallas_call x1, Pallas kernels: 51.9 us -> 48.8 us  [body(): pl.pallas_call(kernel, out_shape=jax.ShapeDtypeStruct(spectral_state.shap...]
where the time goes in v2:
time: 52.1 us; the launch traced here: 51.9 us
  Pallas kernels  48.8 us (94%)
  local copies, waits for them, and re-layouts  3.15 us (6%)
    pallas_call x1, Pallas kernels, body(): pl.pallas_call(kernel, out_shape=jax.ShapeDtypeStruct(spectral_state.shap...  48.8 us
    unnamed x2, local copies, waits for them, and re-layouts  3.15 us

profile of v2, /device:TPU:1, one launch (start us, length us, event | category | flops | bytes accessed | tf_op | source)
XLA Modules:
  0.0 51.9 jit_solution(1483320775207956504)
XLA Ops:
  0.0 1.7 %copy.7.table_hbm = bf16[2,513,128]{2,1,0:T(8,128)(2,1)} copy(bf16[2,513,128]{2,0,1:T(2,128)(2,1)} %param.7) | data formatting | bytes 525312 | tf_op args[1]
  1.7 48.8 %shard_map.64 = f32[2,3,2,2,513]{4,3,2,1,0:T(2,128)} custom-call(f32[2,3,2,2,513]{4,3,2,1,0:T(2,128)} %state_hbm.1, bf16[2,513,128]{2,1,0:T(8,128)(2,1)} %copy.7.table_hbm, s32[1,256]{1,0:T(1,128)} %bitcast.1, s32[256]{0:T(256)} %lows_hbm.1, f32[3]{0:T(128)} %diffusion_hbm.1, f32[3]{0:T(128)} %coupling_hbm.1, bf16[8,384,256]{2,1,0:T(8,128)(2,1)} %constant.2.clone.waves), custom_call_target="tpu_custom_call" | custom-call | tf_op jit(solution)/shard_map/pallas_call | solution.py:350
  50.5 1.5 %copy.9 = f32[2,3,2,2,513]{4,3,2,1,0:T(2,128)} copy(f32[2,3,2,2,513]{4,3,2,1,0:T(2,128)} %shard_map.64) | data formatting | bytes 98496

commit v3 on v2

--- a/solution.py
+++ b/solution.py
@@ -57,7 +57,7 @@
 
 def kernel(
     state_hbm, table_hbm, low_hbm, lows_hbm, diffusion_hbm, coupling_hbm, waves, out,
-    state, table, low_row, lows, diffusion, coupling,
+    state, table, rows, low_row, lows, diffusion, coupling,
     wave_raw, wave_own, masked, st, cg, flat, s1, s2, r1, r2, s3, r3, s4, r4, mid, mid3, inv, send_x, recv_x, total,
     relay, load_sem, sem_cs, sem_cr, sem_1s, sem_1r, sem_2s, sem_2r, sem_3s, sem_3r, sem_4s, sem_4r, sem_us, sem_ur,
 ):
@@ -131,15 +131,16 @@
         ]
 
     loads[4].wait()
+    rows[...] = table[...].astype(F32).reshape(2 * ROWS, 128)
     for p in range(2):
         low = lows[mode * 2 + p]
         low_even = lax.rem(low, 2) == 0
         for start, size in ((0, 512), (512, 128)):
             row = lax.broadcasted_iota(jnp.int32, (size, 128), 0) + start
             if start == 0:
-                values = table[p, 0:512, :].astype(F32)
+                values = rows[pl.ds(p, 512, stride=2), :]
             else:
-                last = table[p, 512:513, :].astype(F32)
+                last = rows[1024 + p : 1025 + p, :]
                 values = jnp.where(row == 512, jnp.broadcast_to(last, (128, 128)), 0.0)
             in_lower = row < ORDERS - low
             even_order = in_lower == low_even
@@ -349,12 +350,13 @@
     dma = pltpu.SemaphoreType.DMA
     return pl.pallas_call(
         kernel,
-        out_shape=jax.ShapeDtypeStruct(spectral_state.shape, F32),
+        out_shape=pltpu.VMEM(spectral_state.shape, F32),
         in_specs=[hbm] * 7,
         out_specs=vmem,
         scratch_shapes=[
             pltpu.VMEM(spectral_state.shape, F32),
-            pltpu.VMEM(synthesis_table.shape, BF16),
+            pltpu.VMEM((ROWS, 2, 128), BF16),
+            pltpu.VMEM((2 * ROWS, 128), F32),
             pltpu.VMEM((1, HALF), jnp.int32),
             pltpu.SMEM((HALF,), jnp.int32),
             pltpu.SMEM((3,), F32),
@@ -391,7 +393,7 @@
         compiler_params=pltpu.CompilerParams(
             collective_id=0, has_side_effects=True, vmem_limit_bytes=63 * 1024 * 1024
         ),
-    )(spectral_state, synthesis_table, low_row, low_orders, diffusion, coupling, jnp.asarray(wave_tables()))
+    )(spectral_state, jnp.transpose(synthesis_table, (1, 0, 2)), low_row, low_orders, diffusion, coupling, jnp.asarray(wave_tables()))
 
 
 def solution(mesh):

time: 52.1 us -> 48.1 us (0.923)
  local copies, waits for them, and re-layouts: 3.15 us -> 0.63 us
  Pallas kernels: 48.8 us -> 47.4 us
    unnamed x2 -> x1, local copies, waits for them, and re-layouts: 3.15 us -> 0.63 us
    pallas_call x1, Pallas kernels: 48.8 us -> 47.4 us  [body(): pl.pallas_call(kernel, out_shape=pltpu.VMEM(spectral_state.shape, F32), i...]
where the time goes in v3:
time: 48.1 us; the launch traced here: 48 us
  Pallas kernels  47.4 us (99%)
  local copies, waits for them, and re-layouts  0.63 us (1%)
    pallas_call x1, Pallas kernels, body(): pl.pallas_call(kernel, out_shape=pltpu.VMEM(spectral_state.shape, F32), i...  47.4 us

profile of v3, /device:TPU:1, one launch (start us, length us, event | category | flops | bytes accessed | tf_op | source)
XLA Modules:
  0.0 48.0 jit_solution(17663157014291776763)
XLA Ops:
  0.0 47.4 %shard_map.64 = f32[2,3,2,2,513]{4,3,2,1,0:T(2,128)S(1)} custom-call(f32[2,3,2,2,513]{4,3,2,1,0:T(2,128)} %state_hbm.1, bf16[513,2,128]{2,1,0:T(2,128)(2,1)} %bitcast.2, s32[1,256]{1,0:T(1,128)} %bitcast.3, s32[256]{0:T(256)} %lows_hbm.1, f32[3]{0:T(128)} %diffusion_hbm.1, f32[3]{0:T(128)} %coupling_hbm.1, bf16[8,384,256]{2,1,0:T(8,128)(2,1)} %constant.2.clone.waves), custom_call_target="tpu_custom_call" | custom-call | tf_op jit(solution)/shard_map/pallas_call | solution.py:351
  47.4 0.6 %copy.8 = f32[2,3,2,2,513]{4,3,2,1,0:T(2,128)} copy(f32[2,3,2,2,513]{4,3,2,1,0:T(2,128)S(1)} %shard_map.64) | data formatting | bytes 98496

commit v4 on v3

--- a/solution.py
+++ b/solution.py
@@ -58,7 +58,7 @@
 def kernel(
     state_hbm, table_hbm, low_hbm, lows_hbm, diffusion_hbm, coupling_hbm, waves, out,
     state, table, rows, low_row, lows, diffusion, coupling,
-    wave_raw, wave_own, masked, st, cg, flat, s1, s2, r1, r2, s3, r3, s4, r4, mid, mid3, inv, send_x, recv_x, total,
+    wave_raw, wave_own, masked, st, cg, flat, s1, s2, r1, r2, s3, r3, s4, r4, mid, mid3, inv, kept, send_x, recv_x, total,
     relay, load_sem, sem_cs, sem_cr, sem_1s, sem_1r, sem_2s, sem_2r, sem_3s, sem_3r, sem_4s, sem_4r, sem_us, sem_ur,
 ):
     slab = lax.axis_index("radial")
@@ -163,17 +163,6 @@
 
     pass_on(0, 2)
 
-    for load in loads[5:]:
-        load.wait()
-    down = lax.broadcasted_iota(jnp.int32, (HALF, HALF), 0)
-    across = lax.broadcasted_iota(jnp.int32, (HALF, HALF), 1)
-    regroup = (down == lax.rem(across, 128) * 2 + across // 128).astype(F32).astype(BF16)
-    natural = jnp.broadcast_to(low_row[...], (HALF, HALF))
-    pick = nn((down == natural).astype(F32).astype(BF16), regroup).astype(BF16)
-    lowest = pick[0:1, :].astype(F32)
-    for q in range(8):
-        wave_own[q] = nn(wave_raw[q], pick).astype(BF16)
-
     pl.semaphore_wait(relay.at[0], 2)
     pass_on(1, 4)
 
@@ -196,37 +185,6 @@
         copy.start()
     r1[near] = s1[near]
 
-    row8 = lax.broadcasted_iota(jnp.int32, (8, PADDED), 0)
-    lane8 = lax.broadcasted_iota(jnp.int32, (8, PADDED), 1)
-    low8 = jnp.where(lax.rem(row8, 2) == 0, lows[mode * 2], lows[mode * 2 + 1])
-    degree = jnp.where(lane8 < ORDERS - low8, low8 + lane8, lane8 - 1).astype(F32)
-    degree = degree * (degree + 1.0) * (shell_step * shell_step)
-    first_shell = row8 < 4
-    for f in range(3):
-        diagonal = []
-        for s in range(8):
-            radius = inner_radius + (s + 0.5) * shell_step
-            diagonal.append(degree * (1.0 / (radius * radius)) + (1.0 / diffusion[f] + 2.0))
-        leading = [jnp.ones((8, PADDED), F32), diagonal[0]]
-        trailing = [jnp.ones((8, PADDED), F32), diagonal[7]]
-        for s in range(1, 8):
-            leading.append(diagonal[s] * leading[s] - leading[s - 1])
-            trailing.append(diagonal[7 - s] * trailing[s] - trailing[s - 1])
-        share = 1.0 / leading[8]
-        scaled = [value * share for value in leading]
-
-        def entry(i, j):
-            return scaled[min(i, j)] * trailing[7 - max(i, j)]
-
-        for i in range(SLABS):
-            for j in range(i, SLABS):
-                inv[f, 0, i, j] = jnp.where(first_shell, entry(2 * i, 2 * j), entry(2 * i + 1, 2 * j + 1))
-                inv[f, 1, i, j] = jnp.where(first_shell, entry(2 * i, 2 * j + 1), entry(2 * i + 1, 2 * j))
-                if i != j:
-                    inv[f, 0, j, i] = jnp.where(first_shell, entry(2 * i, 2 * j), entry(2 * i + 1, 2 * j + 1))
-                    inv[f, 1, j, i] = jnp.where(first_shell, entry(2 * i + 1, 2 * j), entry(2 * i, 2 * j + 1))
-
-
     for copy in hop1:
         copy.wait()
     arrived = r1[...].reshape(128, QUARTER).astype(F32)
@@ -239,6 +197,18 @@
     for copy in hop2:
         copy.start()
     r2[far] = s2[far]
+
+    for load in loads[5:]:
+        load.wait()
+    down = lax.broadcasted_iota(jnp.int32, (HALF, HALF), 0)
+    across = lax.broadcasted_iota(jnp.int32, (HALF, HALF), 1)
+    regroup = (down == lax.rem(across, 128) * 2 + across // 128).astype(F32).astype(BF16)
+    natural = jnp.broadcast_to(low_row[...], (HALF, HALF))
+    pick = nn((down == natural).astype(F32).astype(BF16), regroup).astype(BF16)
+    lowest = pick[0:1, :].astype(F32)
+    for q in range(8):
+        wave_own[q] = nn(wave_raw[q], pick).astype(BF16)
+
 
     for copy in hop2:
         copy.wait()
@@ -294,6 +264,37 @@
     for copy in hop3:
         copy.start()
     r3[far] = s3[far]
+
+    row8 = lax.broadcasted_iota(jnp.int32, (8, PADDED), 0)
+    lane8 = lax.broadcasted_iota(jnp.int32, (8, PADDED), 1)
+    low8 = jnp.where(lax.rem(row8, 2) == 0, lows[mode * 2], lows[mode * 2 + 1])
+    degree = jnp.where(lane8 < ORDERS - low8, low8 + lane8, lane8 - 1).astype(F32)
+    degree = degree * (degree + 1.0) * (shell_step * shell_step)
+    first_shell = row8 < 4
+    for f in range(3):
+        diagonal = []
+        for s in range(8):
+            radius = inner_radius + (s + 0.5) * shell_step
+            diagonal.append(degree * (1.0 / (radius * radius)) + (1.0 / diffusion[f] + 2.0))
+        leading = [jnp.ones((8, PADDED), F32), diagonal[0]]
+        trailing = [jnp.ones((8, PADDED), F32), diagonal[7]]
+        for s in range(1, 8):
+            leading.append(diagonal[s] * leading[s] - leading[s - 1])
+            trailing.append(diagonal[7 - s] * trailing[s] - trailing[s - 1])
+        share = 1.0 / leading[8]
+        scaled = [value * share for value in leading]
+
+        def entry(i, j):
+            return scaled[min(i, j)] * trailing[7 - max(i, j)]
+
+        for i in range(SLABS):
+            for j in range(i, SLABS):
+                inv[f, 0, i, j] = jnp.where(first_shell, entry(2 * i, 2 * j), entry(2 * i + 1, 2 * j + 1))
+                inv[f, 1, i, j] = jnp.where(first_shell, entry(2 * i, 2 * j + 1), entry(2 * i + 1, 2 * j))
+                if i != j:
+                    inv[f, 0, j, i] = jnp.where(first_shell, entry(2 * i, 2 * j), entry(2 * i + 1, 2 * j + 1))
+                    inv[f, 1, j, i] = jnp.where(first_shell, entry(2 * i + 1, 2 * j), entry(2 * i, 2 * j + 1))
+
     for copy in hop3:
         copy.wait()
     mid3[...] = r3[...].astype(F32).reshape(FAR * 24, 128)
@@ -314,6 +315,7 @@
     lhs = jnp.concatenate([flat[b * 96 : (b + 1) * 96, :] for b in range(4)], axis=1).astype(BF16)
     first_pair = lax.rem(lax.broadcasted_iota(jnp.int32, (96, PADDED), 0), 2) == 0
     nonlinear = jnp.where(first_pair, nt(lhs, masked[0]), nt(lhs, masked[1]))
+    values = [[] for _ in range(SLABS)]
     for f in range(3):
         own = st[f * 8 : (f + 1) * 8, :] * (2.0 / diffusion[f])
         drives, swapped = [], []
@@ -327,14 +329,18 @@
             value = inv[f, 0, i, 0] * drives[0] + inv[f, 1, i, 0] * swapped[0]
             for j in range(1, SLABS):
                 value = value + inv[f, 0, i, j] * drives[j] + inv[f, 1, i, j] * swapped[j]
-            send_x[i, f * 8 : (f + 1) * 8, :] = value
+            values[i].append(value)
+    for i in range(SLABS):
+        whole = jnp.concatenate(values[i], axis=0)
+        kept[i] = whole
+        send_x[i] = whole.astype(BF16)
     last = [x_copy(send_x.at[x_peer(X_STEPS[i])], recv_x.at[i], i, sem_us, sem_ur) for i in range(SLABS - 1)]
     for copy in last:
         copy.start()
-    total[...] = send_x[slab] - st[...]
+    total[...] = kept[slab] - st[...]
     for copy in last:
         copy.wait()
-    total[...] = total[...] + recv_x[0] + recv_x[1] + recv_x[2]
+    total[...] = total[...] + recv_x[0].astype(F32) + recv_x[1].astype(F32) + recv_x[2].astype(F32)
     for f in range(3):
         for s in range(2):
             for c in range(2):
@@ -379,7 +385,8 @@
             pltpu.VMEM((FAR * 24, 128), F32),
             pltpu.VMEM((3, 2, SLABS, SLABS, 8, PADDED), F32),
             pltpu.VMEM((SLABS, 24, PADDED), F32),
-            pltpu.VMEM((SLABS - 1, 24, PADDED), F32),
+            pltpu.VMEM((SLABS, 24, PADDED), BF16),
+            pltpu.VMEM((SLABS - 1, 24, PADDED), BF16),
             pltpu.VMEM((24, PADDED), F32),
             pltpu.SemaphoreType.REGULAR((2,)),
             dma((7,)),

time: 48.1 us -> 47.5 us (0.988)
  Pallas kernels: 47.4 us -> 46.7 us
    pallas_call x1, Pallas kernels: 47.4 us -> 46.7 us  [body(): pl.pallas_call(kernel, out_shape=pltpu.VMEM(spectral_state.shape, F32), i...]
where the time goes in v4:
time: 47.5 us; the launch traced here: 47.4 us
  Pallas kernels  46.7 us (98%)
  local copies, waits for them, and re-layouts  0.63 us (1%)
    pallas_call x1, Pallas kernels, body(): pl.pallas_call(kernel, out_shape=pltpu.VMEM(spectral_state.shape, F32), i...  46.7 us

profile of v4, /device:TPU:1, one launch (start us, length us, event | category | flops | bytes accessed | tf_op | source)
XLA Modules:
  0.0 47.4 jit_solution(14041558680072070381)
XLA Ops:
  0.0 46.7 %shard_map.64 = f32[2,3,2,2,513]{4,3,2,1,0:T(2,128)S(1)} custom-call(f32[2,3,2,2,513]{4,3,2,1,0:T(2,128)} %state_hbm.1, bf16[513,2,128]{2,1,0:T(2,128)(2,1)} %bitcast.2, s32[1,256]{1,0:T(1,128)} %bitcast.3, s32[256]{0:T(256)} %lows_hbm.1, f32[3]{0:T(128)} %diffusion_hbm.1, f32[3]{0:T(128)} %coupling_hbm.1, bf16[8,384,256]{2,1,0:T(8,128)(2,1)} %constant.2.clone.waves), custom_call_target="tpu_custom_call" | custom-call | tf_op jit(solution)/shard_map/pallas_call | solution.py:357
  46.8 0.6 %copy.8 = f32[2,3,2,2,513]{4,3,2,1,0:T(2,128)} copy(f32[2,3,2,2,513]{4,3,2,1,0:T(2,128)S(1)} %shard_map.64) | data formatting | bytes 98496

commit v5 on v4

--- a/solution.py
+++ b/solution.py
@@ -25,6 +25,10 @@
 X_STEPS = (2, 1, 3)
 NEAR_STEPS = ((2, 0), (2, 1), (1, 0), (3, 0), (1, 1), (3, 1), (0, 1))
 FAR_STEPS = (8, 7, 9, 6, 10, 5, 11, 4, 12, 3, 13, 2, 14, 1, 15)
+ALL_STEPS = sorted(
+    ((z, y, c) for z in range(FAR) for y in range(4) for c in range(2) if z or y or c),
+    key=lambda step: (-min(step[0], FAR - step[0]) - min(step[1], 4 - step[1]), step),
+)
 GREETED = (2, 14, 1, 15)
 KAPPA = 2.0 * math.sqrt(ORDERS * (ORDERS + 1) / (NLAT * NLON))
 MESH = pl.DeviceIdType.MESH
@@ -58,8 +62,8 @@
 def kernel(
     state_hbm, table_hbm, low_hbm, lows_hbm, diffusion_hbm, coupling_hbm, waves, out,
     state, table, rows, low_row, lows, diffusion, coupling,
-    wave_raw, wave_own, masked, st, cg, flat, s1, s2, r1, r2, s3, r3, s4, r4, mid, mid3, inv, kept, send_x, recv_x, total,
-    relay, load_sem, sem_cs, sem_cr, sem_1s, sem_1r, sem_2s, sem_2r, sem_3s, sem_3r, sem_4s, sem_4r, sem_us, sem_ur,
+    wave_raw, wave_own, masked, st, cg, flat, s1, s2, r1, r2, s3, r3, mid, mid4, inv, send_x, recv_x, total,
+    relay, load_sem, sem_cs, sem_cr, sem_1s, sem_1r, sem_2s, sem_2r, sem_3s, sem_3r, sem_us, sem_ur,
 ):
     slab = lax.axis_index("radial")
     mode = lax.axis_index("mode")
@@ -96,6 +100,7 @@
         load.start()
 
     st[...] = jnp.zeros_like(st)
+    mid4[...] = jnp.zeros_like(mid4)
     for load in loads[:4]:
         load.wait()
     for f in range(3):
@@ -258,12 +263,16 @@
                     flat[pl.ds((h * 2 + q) * 96 + c * 2 + p, 24, stride=4), :] = answer[
                         h * 24 : (h + 1) * 24, p * 128 : (p + 1) * 128
                     ]
-    turned = [flat[g * 128 : (g + 1) * 128, :].T.reshape(FAR, NEAR, 128) for g in range(3)]
-    s3[...] = jnp.concatenate(turned, axis=1).astype(BF16)
-    hop3 = far_copies(s3, r3, sem_3s, sem_3r)
-    for copy in hop3:
-        copy.start()
-    r3[far] = s3[far]
+    for g in range(3):
+        mid4[pl.ds(g, 128, stride=4), :] = flat[g * 128 : (g + 1) * 128, :].T
+    s3[...] = mid4[...].reshape(128, 4, 128).astype(BF16)
+    for z, y, c in ALL_STEPS:
+        peer = far_peer(z) * NEAR + near_peer((y, c))
+        pltpu.make_async_remote_copy(
+            src_ref=s3.at[peer], dst_ref=r3.at[mode], send_sem=sem_3s.at[0], recv_sem=sem_3r.at[0],
+            device_id=(slab, peer), device_id_type=MESH,
+        ).start()
+    r3[mode] = s3[mode]
 
     row8 = lax.broadcasted_iota(jnp.int32, (8, PADDED), 0)
     lane8 = lax.broadcasted_iota(jnp.int32, (8, PADDED), 1)
@@ -295,27 +304,18 @@
                     inv[f, 0, j, i] = jnp.where(first_shell, entry(2 * i, 2 * j), entry(2 * i + 1, 2 * j + 1))
                     inv[f, 1, j, i] = jnp.where(first_shell, entry(2 * i + 1, 2 * j), entry(2 * i, 2 * j + 1))
 
-    for copy in hop3:
-        copy.wait()
-    mid3[...] = r3[...].astype(F32).reshape(FAR * 24, 128)
-    for y in range(NEAR):
-        s4[y] = jnp.concatenate(
-            [mid3[pl.ds(g * 8 + y, FAR, stride=24), :] for g in range(3)], axis=1
-        ).astype(BF16)
-    hop4 = near_copies(s4, r4, sem_4s, sem_4r)
-    for copy in hop4:
-        copy.start()
-    r4[near] = s4[near]
-    for copy in hop4:
-        copy.wait()
-
-    arrived = r4[...].reshape(128, QUARTER).astype(F32)
+    others = len(ALL_STEPS)
+    pltpu.make_async_copy(r3.at[0:others], r3.at[0:others], sem_3r.at[0]).wait()
+    pltpu.make_async_copy(s3.at[0:others], s3.at[0:others], sem_3s.at[0]).wait()
+
+    mid4[...] = r3[...].astype(F32).reshape(512, 128)
     for g in range(3):
-        flat[g * 128 : (g + 1) * 128, :] = arrived[:, g * 128 : (g + 1) * 128].T
+        flat[g * 128 : (g + 1) * 128, :] = jnp.concatenate(
+            [mid4[pl.ds(y * 4 + g, FAR, stride=32), :] for y in range(NEAR)], axis=0
+        ).T
     lhs = jnp.concatenate([flat[b * 96 : (b + 1) * 96, :] for b in range(4)], axis=1).astype(BF16)
     first_pair = lax.rem(lax.broadcasted_iota(jnp.int32, (96, PADDED), 0), 2) == 0
     nonlinear = jnp.where(first_pair, nt(lhs, masked[0]), nt(lhs, masked[1]))
-    values = [[] for _ in range(SLABS)]
     for f in range(3):
         own = st[f * 8 : (f + 1) * 8, :] * (2.0 / diffusion[f])
         drives, swapped = [], []
@@ -329,18 +329,14 @@
             value = inv[f, 0, i, 0] * drives[0] + inv[f, 1, i, 0] * swapped[0]
             for j in range(1, SLABS):
                 value = value + inv[f, 0, i, j] * drives[j] + inv[f, 1, i, j] * swapped[j]
-            values[i].append(value)
-    for i in range(SLABS):
-        whole = jnp.concatenate(values[i], axis=0)
-        kept[i] = whole
-        send_x[i] = whole.astype(BF16)
+            send_x[i, f * 8 : (f + 1) * 8, :] = value
     last = [x_copy(send_x.at[x_peer(X_STEPS[i])], recv_x.at[i], i, sem_us, sem_ur) for i in range(SLABS - 1)]
     for copy in last:
         copy.start()
-    total[...] = kept[slab] - st[...]
+    total[...] = send_x[slab] - st[...]
     for copy in last:
         copy.wait()
-    total[...] = total[...] + recv_x[0].astype(F32) + recv_x[1].astype(F32) + recv_x[2].astype(F32)
+    total[...] = total[...] + recv_x[0] + recv_x[1] + recv_x[2]
     for f in range(3):
         for s in range(2):
             for c in range(2):
@@ -377,24 +373,20 @@
             pltpu.VMEM((FAR, 24, 128), BF16),
             pltpu.VMEM((NEAR, FAR, 384), BF16),
             pltpu.VMEM((FAR, 24, 128), BF16),
-            pltpu.VMEM((FAR, 24, 128), BF16),
-            pltpu.VMEM((FAR, 24, 128), BF16),
-            pltpu.VMEM((NEAR, FAR, 384), BF16),
-            pltpu.VMEM((NEAR, FAR, 384), BF16),
+            pltpu.VMEM((128, 4, 128), BF16),
+            pltpu.VMEM((128, 4, 128), BF16),
             pltpu.VMEM((3, 128, 128), F32),
-            pltpu.VMEM((FAR * 24, 128), F32),
+            pltpu.VMEM((512, 128), F32),
             pltpu.VMEM((3, 2, SLABS, SLABS, 8, PADDED), F32),
             pltpu.VMEM((SLABS, 24, PADDED), F32),
-            pltpu.VMEM((SLABS, 24, PADDED), BF16),
-            pltpu.VMEM((SLABS - 1, 24, PADDED), BF16),
+            pltpu.VMEM((SLABS - 1, 24, PADDED), F32),
             pltpu.VMEM((24, PADDED), F32),
             pltpu.SemaphoreType.REGULAR((2,)),
             dma((7,)),
             dma((SLABS - 1,)), dma((SLABS - 1,)),
             dma((NEAR - 1,)), dma((NEAR - 1,)),
             dma((FAR - 1,)), dma((FAR - 1,)),
-            dma((FAR - 1,)), dma((FAR - 1,)),
-            dma((NEAR - 1,)), dma((NEAR - 1,)),
+            dma((1,)), dma((1,)),
             dma((SLABS - 1,)), dma((SLABS - 1,)),
         ],
         compiler_params=pltpu.CompilerParams(

time: 47.5 us -> 46 us (0.968)
  Pallas kernels: 46.7 us -> 45.2 us
    pallas_call x1, Pallas kernels: 46.7 us -> 45.2 us  [body(): pl.pallas_call(kernel, out_shape=pltpu.VMEM(spectral_state.shape, F32), i...]
where the time goes in v5:
time: 46 us; the launch traced here: 45.9 us
  Pallas kernels  45.2 us (98%)
  local copies, waits for them, and re-layouts  0.63 us (1%)
    pallas_call x1, Pallas kernels, body(): pl.pallas_call(kernel, out_shape=pltpu.VMEM(spectral_state.shape, F32), i...  45.2 us

profile of v5, /device:TPU:1, one launch (start us, length us, event | category | flops | bytes accessed | tf_op | source)
XLA Modules:
  0.0 45.9 jit_solution(15634505285225073406)
XLA Ops:
  0.0 45.2 %shard_map.64 = f32[2,3,2,2,513]{4,3,2,1,0:T(2,128)S(1)} custom-call(f32[2,3,2,2,513]{4,3,2,1,0:T(2,128)} %state_hbm.1, bf16[513,2,128]{2,1,0:T(2,128)(2,1)} %bitcast.2, s32[1,256]{1,0:T(1,128)} %bitcast.3, s32[256]{0:T(256)} %lows_hbm.1, f32[3]{0:T(128)} %diffusion_hbm.1, f32[3]{0:T(128)} %coupling_hbm.1, bf16[8,384,256]{2,1,0:T(8,128)(2,1)} %constant.2.clone.waves), custom_call_target="tpu_custom_call" | custom-call | tf_op jit(solution)/shard_map/pallas_call | solution.py:353
  45.2 0.6 %copy.8 = f32[2,3,2,2,513]{4,3,2,1,0:T(2,128)} copy(f32[2,3,2,2,513]{4,3,2,1,0:T(2,128)S(1)} %shard_map.64) | data formatting | bytes 98496

commit v6 on v5

--- a/solution.py
+++ b/solution.py
@@ -27,7 +27,7 @@
 FAR_STEPS = (8, 7, 9, 6, 10, 5, 11, 4, 12, 3, 13, 2, 14, 1, 15)
 ALL_STEPS = sorted(
     ((z, y, c) for z in range(FAR) for y in range(4) for c in range(2) if z or y or c),
-    key=lambda step: (-min(step[0], FAR - step[0]) - min(step[1], 4 - step[1]), step),
+    key=lambda step: (-min(step[0], FAR - step[0]) - min(step[1], 4 - step[1]), step[::-1]),
 )
 GREETED = (2, 14, 1, 15)
 KAPPA = 2.0 * math.sqrt(ORDERS * (ORDERS + 1) / (NLAT * NLON))
@@ -80,12 +80,12 @@
         return lax.rem(far + step, FAR)
 
     barrier = pltpu.get_barrier_semaphore()
+    for step in X_STEPS:
+        pl.semaphore_signal(barrier, inc=1, device_id=(x_peer(step), mode), device_id_type=MESH)
     for step in GREETED:
         pl.semaphore_signal(barrier, inc=1, device_id=(slab, far_peer(step) * NEAR + near), device_id_type=MESH)
     for step in NEAR_STEPS:
         pl.semaphore_signal(barrier, inc=1, device_id=(slab, far * NEAR + near_peer(step)), device_id_type=MESH)
-    for step in X_STEPS:
-        pl.semaphore_signal(barrier, inc=1, device_id=(x_peer(step), mode), device_id_type=MESH)
 
     loads = [
         pltpu.make_async_copy(source, target, load_sem.at[i])
@@ -316,6 +316,7 @@
     lhs = jnp.concatenate([flat[b * 96 : (b + 1) * 96, :] for b in range(4)], axis=1).astype(BF16)
     first_pair = lax.rem(lax.broadcasted_iota(jnp.int32, (96, PADDED), 0), 2) == 0
     nonlinear = jnp.where(first_pair, nt(lhs, masked[0]), nt(lhs, masked[1]))
+    tails = [[] for _ in range(SLABS)]
     for f in range(3):
         own = st[f * 8 : (f + 1) * 8, :] * (2.0 / diffusion[f])
         drives, swapped = [], []
@@ -329,14 +330,25 @@
             value = inv[f, 0, i, 0] * drives[0] + inv[f, 1, i, 0] * swapped[0]
             for j in range(1, SLABS):
                 value = value + inv[f, 0, i, j] * drives[j] + inv[f, 1, i, j] * swapped[j]
-            send_x[i, f * 8 : (f + 1) * 8, :] = value
+            for t in range(4):
+                send_x[i, (f * 4 + t) * 8 : (f * 4 + t + 1) * 8, :] = value[:, t * 128 : (t + 1) * 128]
+            tails[i].append(value[:, 512:PADDED])
+    lane = lax.broadcasted_iota(jnp.int32, (8, 128), 1)
+    for i in range(SLABS):
+        send_x[i, 96:104, :] = jnp.where(
+            lane == 0, tails[i][0], jnp.where(lane == 1, pltpu.roll(tails[i][1], 1, 1), pltpu.roll(tails[i][2], 2, 1))
+        )
     last = [x_copy(send_x.at[x_peer(X_STEPS[i])], recv_x.at[i], i, sem_us, sem_ur) for i in range(SLABS - 1)]
     for copy in last:
         copy.start()
-    total[...] = send_x[slab] - st[...]
     for copy in last:
         copy.wait()
-    total[...] = total[...] + recv_x[0] + recv_x[1] + recv_x[2]
+    whole = send_x[slab] + recv_x[0] + recv_x[1] + recv_x[2]
+    for f in range(3):
+        for t in range(4):
+            tile = whole[(f * 4 + t) * 8 : (f * 4 + t + 1) * 8]
+            total[f * 8 : (f + 1) * 8, t * 128 : (t + 1) * 128] = tile - st[f * 8 : (f + 1) * 8, t * 128 : (t + 1) * 128]
+        total[f * 8 : (f + 1) * 8, 512:513] = whole[96:104, f : f + 1] - st[f * 8 : (f + 1) * 8, 512:513]
     for f in range(3):
         for s in range(2):
             for c in range(2):
@@ -378,8 +390,8 @@
             pltpu.VMEM((3, 128, 128), F32),
             pltpu.VMEM((512, 128), F32),
             pltpu.VMEM((3, 2, SLABS, SLABS, 8, PADDED), F32),
-            pltpu.VMEM((SLABS, 24, PADDED), F32),
-            pltpu.VMEM((SLABS - 1, 24, PADDED), F32),
+            pltpu.VMEM((SLABS, 104, 128), F32),
+            pltpu.VMEM((SLABS - 1, 104, 128), F32),
             pltpu.VMEM((24, PADDED), F32),
             pltpu.SemaphoreType.REGULAR((2,)),
             dma((7,)),

time: 46 us -> 45.9 us (level)
  no operation moved by 1% of the time
where the time goes in v6:
time: 45.9 us; the launch traced here: 45.8 us
  Pallas kernels  45.1 us (98%)
  local copies, waits for them, and re-layouts  0.63 us (1%)
    pallas_call x1, Pallas kernels, body(): pl.pallas_call(kernel, out_shape=pltpu.VMEM(spectral_state.shape, F32), i...  45.1 us

profile of v6, /device:TPU:1, one launch (start us, length us, event | category | flops | bytes accessed | tf_op | source)
XLA Modules:
  0.0 45.8 jit_solution(17270863599290798657)
XLA Ops:
  0.0 45.1 %shard_map.64 = f32[2,3,2,2,513]{4,3,2,1,0:T(2,128)S(1)} custom-call(f32[2,3,2,2,513]{4,3,2,1,0:T(2,128)} %state_hbm.1, bf16[513,2,128]{2,1,0:T(2,128)(2,1)} %bitcast.2, s32[1,256]{1,0:T(1,128)} %bitcast.3, s32[256]{0:T(256)} %lows_hbm.1, f32[3]{0:T(128)} %diffusion_hbm.1, f32[3]{0:T(128)} %coupling_hbm.1, bf16[8,384,256]{2,1,0:T(8,128)(2,1)} %constant.2.clone.waves), custom_call_target="tpu_custom_call" | custom-call | tf_op jit(solution)/shard_map/pallas_call | solution.py:365
  45.1 0.6 %copy.8 = f32[2,3,2,2,513]{4,3,2,1,0:T(2,128)} copy(f32[2,3,2,2,513]{4,3,2,1,0:T(2,128)S(1)} %shard_map.64) | data formatting | bytes 98496

commit v7 on v5

--- a/solution.py
+++ b/solution.py
@@ -316,6 +316,7 @@
     lhs = jnp.concatenate([flat[b * 96 : (b + 1) * 96, :] for b in range(4)], axis=1).astype(BF16)
     first_pair = lax.rem(lax.broadcasted_iota(jnp.int32, (96, PADDED), 0), 2) == 0
     nonlinear = jnp.where(first_pair, nt(lhs, masked[0]), nt(lhs, masked[1]))
+    last = []
     for f in range(3):
         own = st[f * 8 : (f + 1) * 8, :] * (2.0 / diffusion[f])
         drives, swapped = [], []
@@ -329,14 +330,20 @@
             value = inv[f, 0, i, 0] * drives[0] + inv[f, 1, i, 0] * swapped[0]
             for j in range(1, SLABS):
                 value = value + inv[f, 0, i, j] * drives[j] + inv[f, 1, i, j] * swapped[j]
-            send_x[i, f * 8 : (f + 1) * 8, :] = value
-    last = [x_copy(send_x.at[x_peer(X_STEPS[i])], recv_x.at[i], i, sem_us, sem_ur) for i in range(SLABS - 1)]
-    for copy in last:
-        copy.start()
-    total[...] = send_x[slab] - st[...]
+            send_x[i, f] = value
+        for i in range(SLABS - 1):
+            last.append(
+                pltpu.make_async_remote_copy(
+                    src_ref=send_x.at[x_peer(X_STEPS[i]), f], dst_ref=recv_x.at[i, f],
+                    send_sem=sem_us.at[f * 3 + i], recv_sem=sem_ur.at[f * 3 + i],
+                    device_id=(x_peer(X_STEPS[i]), mode), device_id_type=MESH,
+                )
+            )
+            last[-1].start()
+    total[...] = send_x[slab].reshape(24, PADDED) - st[...]
     for copy in last:
         copy.wait()
-    total[...] = total[...] + recv_x[0] + recv_x[1] + recv_x[2]
+    total[...] = total[...] + (recv_x[0] + recv_x[1] + recv_x[2]).reshape(24, PADDED)
     for f in range(3):
         for s in range(2):
             for c in range(2):
@@ -378,8 +385,8 @@
             pltpu.VMEM((3, 128, 128), F32),
             pltpu.VMEM((512, 128), F32),
             pltpu.VMEM((3, 2, SLABS, SLABS, 8, PADDED), F32),
-            pltpu.VMEM((SLABS, 24, PADDED), F32),
-            pltpu.VMEM((SLABS - 1, 24, PADDED), F32),
+            pltpu.VMEM((SLABS, 3, 8, PADDED), F32),
+            pltpu.VMEM((SLABS - 1, 3, 8, PADDED), F32),
             pltpu.VMEM((24, PADDED), F32),
             pltpu.SemaphoreType.REGULAR((2,)),
             dma((7,)),
@@ -387,7 +394,7 @@
             dma((NEAR - 1,)), dma((NEAR - 1,)),
             dma((FAR - 1,)), dma((FAR - 1,)),
             dma((1,)), dma((1,)),
-            dma((SLABS - 1,)), dma((SLABS - 1,)),
+            dma((9,)), dma((9,)),
         ],
         compiler_params=pltpu.CompilerParams(
             collective_id=0, has_side_effects=True, vmem_limit_bytes=63 * 1024 * 1024

time: 46 us -> 46.5 us (1.011)
  Pallas kernels: 45.2 us -> 45.7 us
    pallas_call x1, Pallas kernels: 45.2 us -> 45.7 us  [body(): pl.pallas_call(kernel, out_shape=pltpu.VMEM(spectral_state.shape, F32), i...]
where the time goes in v7:
time: 46.5 us; the launch traced here: 46.4 us
  Pallas kernels  45.7 us (98%)
  local copies, waits for them, and re-layouts  0.63 us (1%)
    pallas_call x1, Pallas kernels, body(): pl.pallas_call(kernel, out_shape=pltpu.VMEM(spectral_state.shape, F32), i...  45.7 us

profile of v7, /device:TPU:1, one launch (start us, length us, event | category | flops | bytes accessed | tf_op | source)
XLA Modules:
  0.0 46.4 jit_solution(14047552658836108494)
XLA Ops:
  0.0 45.7 %shard_map.64 = f32[2,3,2,2,513]{4,3,2,1,0:T(2,128)S(1)} custom-call(f32[2,3,2,2,513]{4,3,2,1,0:T(2,128)} %state_hbm.1, bf16[513,2,128]{2,1,0:T(2,128)(2,1)} %bitcast.2, s32[1,256]{1,0:T(1,128)} %bitcast.3, s32[256]{0:T(256)} %lows_hbm.1, f32[3]{0:T(128)} %diffusion_hbm.1, f32[3]{0:T(128)} %coupling_hbm.1, bf16[8,384,256]{2,1,0:T(8,128)(2,1)} %constant.2.clone.waves), custom_call_target="tpu_custom_call" | custom-call | tf_op jit(solution)/shard_map/pallas_call | solution.py:360
  45.7 0.6 %copy.8 = f32[2,3,2,2,513]{4,3,2,1,0:T(2,128)} copy(f32[2,3,2,2,513]{4,3,2,1,0:T(2,128)S(1)} %shard_map.64) | data formatting | bytes 98496

commit v8 on v5

--- a/solution.py
+++ b/solution.py
@@ -172,7 +172,7 @@
     pass_on(1, 4)
 
     for copy in coefs:
-        copy.wait()
+        copy.wait_recv()
 
     gathered = [cg[i].astype(F32) for i in range(SLABS)]
     lhs = jnp.concatenate(
@@ -191,7 +191,7 @@
     r1[near] = s1[near]
 
     for copy in hop1:
-        copy.wait()
+        copy.wait_recv()
     arrived = r1[...].reshape(128, QUARTER).astype(F32)
     for g in range(3):
         mid[g] = arrived[:, g * 128 : (g + 1) * 128]
@@ -216,7 +216,7 @@
 
 
     for copy in hop2:
-        copy.wait()
+        copy.wait_recv()
     arrived = r2[...].astype(F32)
     for g in range(3):
         flat[g * 128 : (g + 1) * 128, :] = arrived[:, g * 8 : (g + 1) * 8, :].reshape(128, 128).T
@@ -306,7 +306,6 @@
 
     others = len(ALL_STEPS)
     pltpu.make_async_copy(r3.at[0:others], r3.at[0:others], sem_3r.at[0]).wait()
-    pltpu.make_async_copy(s3.at[0:others], s3.at[0:others], sem_3s.at[0]).wait()
 
     mid4[...] = r3[...].astype(F32).reshape(512, 128)
     for g in range(3):
@@ -335,7 +334,7 @@
         copy.start()
     total[...] = send_x[slab] - st[...]
     for copy in last:
-        copy.wait()
+        copy.wait_recv()
     total[...] = total[...] + recv_x[0] + recv_x[1] + recv_x[2]
     for f in range(3):
         for s in range(2):
@@ -343,6 +342,9 @@
                 for p in range(2):
                     row = f * 8 + s * 4 + c * 2 + p
                     out[p, f, s, c : c + 1, :] = total[row : row + 1, 0:ROWS]
+    for copy in coefs + hop1 + hop2 + last:
+        copy.wait_send()
+    pltpu.make_async_copy(s3.at[0:others], s3.at[0:others], sem_3s.at[0]).wait()
 
 
 def body(spectral_state, synthesis_table, low_orders, diffusion, coupling):

time: 46 us -> 46 us (level)
  no operation moved by 1% of the time
where the time goes in v8:
time: 46 us; the launch traced here: 45.9 us
  Pallas kernels  45.3 us (98%)
  local copies, waits for them, and re-layouts  0.63 us (1%)
    pallas_call x1, Pallas kernels, body(): pl.pallas_call(kernel, out_shape=pltpu.VMEM(spectral_state.shape, F32), i...  45.3 us

profile of v8, /device:TPU:1, one launch (start us, length us, event | category | flops | bytes accessed | tf_op | source)
XLA Modules:
  0.0 45.9 jit_solution(4430373860303073557)
XLA Ops:
  0.0 45.3 %shard_map.64 = f32[2,3,2,2,513]{4,3,2,1,0:T(2,128)S(1)} custom-call(f32[2,3,2,2,513]{4,3,2,1,0:T(2,128)} %state_hbm.1, bf16[513,2,128]{2,1,0:T(2,128)(2,1)} %bitcast.2, s32[1,256]{1,0:T(1,128)} %bitcast.3, s32[256]{0:T(256)} %lows_hbm.1, f32[3]{0:T(128)} %diffusion_hbm.1, f32[3]{0:T(128)} %coupling_hbm.1, bf16[8,384,256]{2,1,0:T(8,128)(2,1)} %constant.2.clone.waves), custom_call_target="tpu_custom_call" | custom-call | tf_op jit(solution)/shard_map/pallas_call | solution.py:355
  45.3 0.6 %copy.8 = f32[2,3,2,2,513]{4,3,2,1,0:T(2,128)} copy(f32[2,3,2,2,513]{4,3,2,1,0:T(2,128)S(1)} %shard_map.64) | data formatting | bytes 98496
